TPU v7x, 256 devices: a whole 4x4x8 slice. The times are simulated.
256 devices in a mesh: row: 8 (over y_lo, x), col: 32 (over y_hi, z, core).
Axes of the slice: x: 4, y: 4 (y_hi: 2, y_lo: 2; y = y_hi * 2 + y_lo), z: 8, core: 2. Of those that a mesh axis runs over, the one named last changes fastest.
Arguments:
- cov: bfloat16 [16384, 16384], P('row', 'col'), as said below
- jac_blocks: bfloat16 [256, 128, 128], P('col'), may hold values from -0.25 to 0.25
- block_positions: int32 [256, 2], P('col'), may hold values from 0 to 127, as said below
- block_counts: int32 [32], P('col'), may hold values from 1 to 8, as said below
- lower_cross_block: float32 [512, 512], replicated, may hold values from -0.25 to 0.25
- pivot_inverse: float32 [2, 512, 512], replicated, as said below
Outputs:
- updated_cov: bfloat16 [16384, 16384], P('row', 'col')
Inputs may be any that keep to these rules, and one draw needn't show every extreme that they name: `block_positions`: block coordinates: column 0 is a measurement block below 8, column 1 a cell block that belongs to the slot's own index of col (slots of index c hold cell blocks c * 4 to (c + 1) * 4 - 1); no pair repeats among the live slots. `block_counts`: some index of col holds exactly 8 live blocks. `cov`: Symmetric. `pivot_inverse`: Symmetric.
All inputs are finite; a program needn't handle non-finite values.
Results may differ from a plain program's by a relative error of at most 0.0063.
Values may be sent and summed in bfloat16 or wider, within the bound.
A program may use at most 128 MiB of HBM per device.

v0:
```python
import jax
import jax.numpy as jnp
from jax import lax
from jax.sharding import PartitionSpec as P


def place(strip, values, block_of_rows, cell_block, first, width):
    local = cell_block - first
    inside = (local >= 0) & (local < width)
    rows_out = jnp.where(inside, block_of_rows, strip.shape[0])
    local = jnp.clip(local, 0, width - 1)
    return strip.at[rows_out, local].add(values, mode="drop")


def to_matrix(strip):
    blocks_m, blocks_c, size_m, size_c = strip.shape
    return strip.transpose(0, 2, 1, 3).reshape(blocks_m * size_m, blocks_c * size_c)


def solve_rows(shares, lower_cross_block, pivot_inverse):
    highest = lax.Precision.HIGHEST
    panel = lower_cross_block.shape[0]
    values = shares.astype(jnp.float32)
    first = values[:, :panel]
    second = values[:, panel:]
    reduced = second - jnp.dot(first, lower_cross_block.T, precision=highest)
    scaled_one = jnp.dot(first, pivot_inverse[0].T, precision=highest)
    scaled_two = jnp.dot(reduced, pivot_inverse[1].T, precision=highest)
    top = scaled_one - jnp.dot(scaled_two, lower_cross_block, precision=highest)
    return jnp.concatenate([top, scaled_two], axis=1).astype(jnp.bfloat16)


def body(cov, jac_blocks, block_positions, block_counts, lower_cross_block, pivot_inverse):
    rows_per_tile, tile_cols = cov.shape
    sparse_block = jac_blocks.shape[1]
    measurement_index = 2 * lower_cross_block.shape[0]
    measurement_block_count = measurement_index // sparse_block
    row_place = lax.axis_index("row")
    col_place = lax.axis_index("col")
    capacity = jac_blocks.shape[0]
    active_slots = jnp.arange(capacity, dtype=jnp.int32) < block_counts[0]
    block_of_rows = jnp.where(active_slots, block_positions[:, 0], measurement_block_count)
    marked = jnp.stack([block_of_rows, block_positions[:, 1]], axis=1)
    columns_wide = tile_cols // sparse_block
    resident_strip = jnp.zeros(
        (measurement_block_count, columns_wide, sparse_block, sparse_block), jnp.bfloat16
    )
    resident_strip = place(
        resident_strip,
        jac_blocks,
        block_of_rows,
        block_positions[:, 1],
        col_place * columns_wide,
        columns_wide,
    )
    jac_cols = to_matrix(resident_strip)
    rows_wide = rows_per_tile // sparse_block
    first_rows = row_place * rows_wide
    blank_strip = jnp.zeros(
        (measurement_block_count, rows_wide, sparse_block, sparse_block), jnp.bfloat16
    )
    values = lax.all_gather(jac_blocks, "col", axis=0, tiled=True)
    coords = lax.all_gather(marked, "col", axis=0, tiled=True)
    row_strip = place(blank_strip, values, coords[:, 0], coords[:, 1], first_rows, rows_wide)
    partial_columns = jnp.dot(to_matrix(row_strip), cov, preferred_element_type=jnp.float32)
    measurement_columns = lax.psum(partial_columns, "row").astype(jnp.bfloat16)
    rows_here = cov
    shares = lax.psum_scatter(
        lax.dot_general(
            rows_here, jac_cols, (((1,), (1,)), ((), ())), preferred_element_type=jnp.float32
        ),
        "col",
        scatter_dimension=0,
        tiled=True,
    ).astype(jnp.bfloat16)
    gains = solve_rows(shares, lower_cross_block, pivot_inverse)
    refresh_gains = lax.all_gather(gains, "col", axis=0, tiled=True)
    rows_here = cov
    covariance_delta = jnp.dot(
        refresh_gains, measurement_columns, preferred_element_type=jnp.float32
    )
    return (rows_here.astype(jnp.float32) - covariance_delta).astype(jnp.bfloat16)


def solution(mesh):
    return jax.shard_map(
        body,
        mesh=mesh,
        in_specs=(P("row", "col"), P("col", None, None), P("col", None), P("col"), P(), P()),
        out_specs=P("row", "col"),
        check_vma=False,
    )
```

profile of v0, /device:TPU:8, one launch (start us, length us, event | category | flops | bytes accessed | tf_op | source)
XLA Modules:
  0.0 436.4 jit_solution(4352815985498408935)
XLA Ops:
  6.5 0.0 copy-start
  6.5 0.0 reduce-scatter.4.cloned.1.call-start
  7.3 0.8 fusion.17
  8.1 0.2 broadcast_in_dim.19
  8.3 2.2 scatter_fusion
  10.5 0.7 copy.10
  11.2 7.2 %convolution_bitcast_fusion = f32[2048,1024]{0,1:T(8,128)} fusion(bf16[2048,512]{1,0:T(8,128)(2,1)} %param.6, bf16[64,8,8,128]{3,2,1,0:T(8,128)(2,1)S(1)} %bitcast.46), kind=kOutput, calls=%fused_computation.2 | convolution fusion | flops 2147483648 | bytes 11534336 | tf_op jit(solution)/shard_map/dot_general | solution.py:69
  18.4 9.3 %copy.14 = f32[2048,1024]{1,0:T(8,128)} copy(f32[2048,1024]{0,1:T(8,128)} %convolution_bitcast_fusion) | data formatting | bytes 16777216
  27.7 0.0 reduce-scatter.4.cloned.1.call-update
  27.7 0.0 all-gather.6.cloned.1.call-start
  27.8 0.7 all-gather.6.cloned.1.call-update
  28.5 0.0 all-gather.4.cloned.1.call-start
  28.5 155.7 %reduce-scatter.4.cloned.1.call-done = f32[64,1024]{1,0:T(8,128)} async-done(((f32[2048,1024]{1,0:T(8,128)}), f32[64,1024]{1,0:T(8,128)}) %reduce-scatter.4.cloned.1.call-update) | async-done | bytes 262160 | tf_op jit(solution)/shard_map/reduce_scatter | solution.py:68
  184.2 1.0 convert_element_type.15
  185.2 0.7 convolution_subtract_fusion.1
  185.9 0.0 copy-done.1
  185.9 0.7 fusion.8
  186.5 1.1 fusion.18
  187.7 0.8 fusion.3
  188.4 0.7 pad_maximum_fusion
  189.1 0.0 all-gather.4.cloned.1.call-update
  189.1 39.3 %all-gather = s32[32,8,2]{1,2,0:T(2,128)S(1)} all-gather(s32[1,8,2]{1,2,0:T(2,128)S(1)} %add_bitcast_fusion), channel_id=1, replica_groups=mesh['row'=8,'col'=32] {'col'}, dimensions={0}, use_global_device_ids=true | all-gather | bytes 2112 | tf_op jit(solution)/shard_map/all_gather | solution.py:63
  228.5 0.1 reshape.29
  228.6 57.9 %all-gather.6.cloned.1.call-done = bf16[256,128,128]{2,1,0:T(8,128)(2,1)} async-done(((bf16[8,128,128]{2,1,0:T(8,128)(2,1)}), bf16[256,128,128]{2,1,0:T(8,128)(2,1)}) %all-gather.6.cloned.1.call-update) | async-done | bytes 8388624 | tf_op jit(solution)/shard_map/all_gather | solution.py:62
  286.5 3.0 broadcast_in_dim.21
  289.5 51.9 %scatter_fusion.1 = bf16[8,16,128,128]{3,2,1,0:T(8,128)(2,1)} fusion(bf16[8,16,128,128]{3,2,1,0:T(8,128)(2,1)} %broadcast_in_dim.21, s32[256]{0:T(256)S(1)} %bitcast.43, bf16[256,128,128]{2,1,0:T(8,128)(2,1)} %all-gather.6.cloned.1.call-done), kind=kCustom, calls=%fused_computation.1 | custom fusion | flops 4194304 | bytes 25167872 | tf_op jit(solution)/shard_map/scatter-add | solution.py:12
  341.4 0.0 copy-start.2
  341.4 5.1 %copy.13 = bf16[8,128,16,128]{3,2,1,0:T(8,128)(2,1)S(1)} copy(bf16[8,128,16,128]{3,1,2,0:T(8,128)(2,1)} %bitcast.42) | data formatting | bytes 8388608 | tf_op jit(solution)/shard_map/transpose | solution.py:17
  346.5 0.0 copy-done.2
  346.5 2.3 fusion
  348.8 74.2 %all-reduce.1 = bf16[1024,512]{1,0:T(8,128)(2,1)} all-reduce(f32[1024,512]{1,0:T(8,128)S(1)} %fusion), channel_id=1, replica_groups=mesh['row'=8,'col'=32] {'row'}, use_global_device_ids=true, to_apply=%region_3.4 | all-reduce | flops 524288 | bytes 3145728 | tf_op jit(solution)/shard_map/psum | solution.py:66
  423.0 6.8 %subtract_convert_fusion = bf16[2048,512]{1,0:T(8,128)(2,1)} fusion(bf16[2048,512]{1,0:T(8,128)(2,1)} %param.6, bf16[2048,1024]{1,0:T(8,128)(2,1)} %all-gather.4.cloned.1.call-done, bf16[1024,512]{1,0:T(8,128)(2,1)} %all-reduce.1), kind=kOutput, calls=%fused_computation.6 | convolution fusion | flops 2150629376 | bytes 9437184 | tf_op jit(solution)/shard_map/dot_general | solution.py:79
  (6 shorter events, 0.0 us)
Async XLA Ops:
  6.5 178.7 %copy-start = (f32[512,512]{1,0:T(8,128)S(1)}, f32[512,512]{1,0:T(8,128)}, u32[]{:S(2)}) copy-start(f32[512,512]{1,0:T(8,128)} %param.10) | copy-start | bytes 3145732
  6.5 177.7 %reduce-scatter.4.cloned.1.call-start = ((), (), s32[]{:S(2)}) async-start(), calls=%async_computation.3 | async-start | bytes 8650752 | tf_op jit(solution)/shard_map/reduce_scatter | solution.py:68
  27.7 158.2 %copy-start.1 = (f32[2,512,512]{2,1,0:T(8,128)S(1)}, f32[2,512,512]{2,1,0:T(8,128)}, u32[]{:S(2)}) copy-start(f32[2,512,512]{2,1,0:T(8,128)} %param.11) | copy-start | bytes 6291460
  27.7 258.8 %all-gather.6.cloned.1.call-start = ((), (), s32[]{:S(2)}) async-start(), calls=%async_computation.2 | async-start | bytes 8650752 | tf_op jit(solution)/shard_map/all_gather | solution.py:62
  28.5 394.5 %all-gather.4.cloned.1.call-start = ((), (), s32[]{:S(2)}) async-start(), calls=%async_computation.1 | async-start | bytes 4325376 | tf_op jit(solution)/shard_map/all_gather | solution.py:77
  341.4 5.1 %copy-start.2 = (bf16[2048,512]{1,0:T(8,128)(2,1)S(1)}, bf16[2048,512]{1,0:T(8,128)(2,1)}, u32[]{:S(2)}) copy-start(bf16[2048,512]{1,0:T(8,128)(2,1)} %param.6) | copy-start | bytes 6291460
Sparse Core Ops, SparseCore 0:
  27.8 156.3 reduce-scatter.3
  187.0 99.4 all-gather.5
  289.3 83.1 all-gather.3
where the time goes:
time: 437 us; the launch traced here: 436 us
  waiting for transfers between devices  214 us (49%)
  blocking collectives  114 us (26%)
  other arithmetic  56.5 us (13%)
  matrix products  19.6 us (4%)
  local copies, waits for them, and re-layouts  18.4 us (4%)
  between operations  13.9 us (3%)
    reduce_scatter x1, waiting for transfers between devices, body(): lax.psum_scatter(lax.dot_general(rows_here, jac_cols, (((1,), (1,)), ((),...  156 us
    psum x1, blocking collectives, body(): measurement_columns = lax.psum(partial_columns, 'row').astype(jnp.bfloat16)  74.2 us
    all_gather x1, waiting for transfers between devices, body(): values = lax.all_gather(jac_blocks, 'col', axis=0, tiled=True)  57.9 us
    scatter-add x2, other arithmetic, place(): return strip.at[rows_out, local].add(values, mode='drop')  54.1 us
    all_gather x1, blocking collectives, body(): coords = lax.all_gather(marked, 'col', axis=0, tiled=True)  39.3 us
    unnamed x8, local copies, waits for them, and re-layouts  9.36 us
  transfers between devices with their start and end apart: 3, of which 2 were waited for; matrix products, arithmetic and copies ran while one was open for 15% of the time, Pallas kernels for 0%

commit v1 on v0

v1 whole, which is shorter than its diff:
```python
import jax
import jax.numpy as jnp
from jax import lax
from jax.experimental import pallas as pl
from jax.experimental.pallas import tpu as pltpu
from jax.sharding import PartitionSpec as P

MESH = pl.DeviceIdType.MESH
F32 = jnp.float32
BF16 = jnp.bfloat16


def dot(a, b):
    return jnp.dot(a, b, preferred_element_type=F32)


def split(values):
    high = values.astype(BF16)
    return high, (values - high.astype(F32)).astype(BF16)


def kernel(
    jac, pos, cnt, cov_hbm, lower, pivot, out,
    cov, jz, tz, jr, tr, table, lhs, psend, pown, rbuf, yb, xt, xb, fac, wb,
    cov_sem, tab_sem,
    z_s, z_r, zt_s, zt_r, p_s, p_r, pt_s, pt_r, d_s, d_r, dt_s, dt_r,
    r_s, r_r, y_s, y_r, a_s, a_r, h_s, h_r, s_s, s_r, u_s, u_r, v_s, v_r,
):
    r = lax.axis_index("row")
    c = lax.axis_index("col")
    y = c // 16
    z = (c // 2) % 8
    q = c % 2
    yl = r // 4
    x = r % 4
    b = c // 4
    j = c % 4

    def col(y_, z_, q_):
        return (y_ * 8 + z_) * 2 + q_

    def remote(src, dst, ss, rs, dev):
        return pltpu.make_async_remote_copy(
            src_ref=src, dst_ref=dst, send_sem=ss, recv_sem=rs, device_id=dev, device_id_type=MESH
        )

    cov_copy = pltpu.make_async_copy(cov_hbm, cov, cov_sem)
    cov_copy.start()

    sub = lax.broadcasted_iota(jnp.int32, (8, 128), 0)
    lane = lax.broadcasted_iota(jnp.int32, (8, 128), 1)
    t = jnp.full((8, 128), 8, jnp.int32)
    for s in range(8):
        hit = (sub == pos[s, 0]) & (lane == pos[s, 1] - c * 4) & (s < cnt[0])
        t = jnp.where(hit, s, t)
    tz[z] = t
    jz[z] = jac[r]

    def z_copy(zz, i):
        return remote(jac.at[r], jz.at[z], z_s.at[i], z_r.at[z], (r, col(y, zz, q)))

    def zt_copy(zz, i):
        return remote(tz.at[z], tz.at[z], zt_s.at[i], zt_r.at[z], (r, col(y, zz, q)))

    @pl.loop(1, 8)
    def _(i):
        zz = lax.rem(z + i, 8)
        z_copy(zz, i).start()
        zt_copy(zz, i).start()

    jr[32] = jnp.zeros((128, 128), BF16)
    for n, value in enumerate((lower[...], lower[...].T, pivot[0], pivot[1])):
        high, low = split(value)
        fac[n, 0] = high
        fac[n, 1] = low

    @pl.loop(0, 4)
    def _(i):
        xx = lax.rem(z // 2 + i, 4)
        for h in range(2):
            zz = 2 * xx + h

            @pl.when(zz != z)
            def _():
                remote(jac.at[r], jz.at[zz], z_s.at[0], z_r.at[zz], (r, c)).wait_recv()
                remote(tz.at[zz], tz.at[zz], zt_s.at[0], zt_r.at[zz], (r, c)).wait_recv()

        to = 4 * y + xx
        for yy in range(2):
            here = (to == r) & (yy == y)

            @pl.when(jnp.logical_not(here))
            def _():
                remote(
                    jz.at[pl.ds(2 * xx, 2)], jr.at[pl.ds((q * 8 + r) * 2, 2)],
                    p_s.at[i * 2 + yy], p_r.at[r], (to, col(yy, z, q)),
                ).start()

            @pl.when(here)
            def _():
                jr[pl.ds((q * 8 + r) * 2, 2)] = jz[pl.ds(2 * xx, 2)]

        @pl.when(to == r)
        def _():
            tr[q] = tz[pl.ds(2 * xx, 2)]
            remote(tz.at[pl.ds(2 * xx, 2)], tr.at[q], pt_s, pt_r, (r, col(1 - y, z, q))).start()

    sib = (r, col(y, z, 1 - q))

    @pl.when(yl != y)
    def _():
        remote(tz.at[pl.ds(0, 2)], tr.at[q], pt_s, pt_r, (r, c)).wait_recv()

    dt = remote(tr.at[q], tr.at[q], dt_s, dt_r, sib)
    dt.start()

    def p_wait(k):
        remote(jz.at[pl.ds(0, 2)], jr.at[pl.ds((q * 8 + k) * 2, 2)], p_s.at[0], p_r.at[k], (r, c)).wait_recv()

    def d_copy(k, side):
        part = jr.at[pl.ds((side * 8 + k) * 2, 2)]
        return remote(part, part, d_s.at[k], d_r.at[k], sib)

    @pl.loop(0, 8)
    def _(i):
        k = lax.rem(r + i, 8)

        @pl.when(jnp.logical_not((k == r) & (yl == y)))
        def _():
            p_wait(k)

        d_copy(k, q).start()

    remote(tr.at[q], tr.at[1 - q], dt_s, dt_r, sib).wait_recv()
    tab_copy = pltpu.make_async_copy(tr, table, tab_sem)
    tab_copy.start()
    tab_copy.wait()

    @pl.loop(0, 8)
    def _(k):
        d_copy(k, 1 - q).wait_recv()

    cov_copy.wait()

    @pl.loop(0, 4)
    def _(i):
        g = lax.rem(r // 2 + 1 + i, 4)
        for h in range(2):
            k = 2 * g + h
            for bb in range(2):
                for qq in range(2):
                    for l in range(4):
                        at = table[qq, bb, k, l]
                        at = jnp.where(at < 8, (qq * 8 + at) * 2 + bb, 32)
                        place = ((2 * bb + qq) * 4 + l) * 128
                        lhs[pl.ds(h * 128, 128), pl.ds(place, 128)] = jr[at]
        part = dot(lhs[...], cov[...])
        for h in range(2):
            k = 2 * g + h

            @pl.when(k == r)
            def _():
                pown[...] = part[h * 128:(h + 1) * 128]

            @pl.when(k != r)
            def _():
                psend[k] = part[h * 128:(h + 1) * 128].astype(BF16)
                remote(psend.at[k], rbuf.at[r], r_s.at[k], r_r.at[r], (k, c)).start()

    @pl.loop(1, 8)
    def _(i):
        k = lax.rem(r + 8 - i, 8)
        remote(psend.at[0], rbuf.at[k], r_s.at[0], r_r.at[k], (r, c)).wait_recv()
        pown[...] += rbuf[k].astype(F32)

    mine = pown[...]
    yb[r] = mine.astype(BF16)
    xt[...] = mine.T.astype(BF16)

    def xi(yy, zz, qq):
        return (zz * 2 + qq) * 2 + yy

    strip = pl.ds(pl.multiple_of(r * 128, 128), 128)
    own = xi(y, z, q)

    @pl.loop(0, 8)
    def _(i_):
        i = lax.rem(r + i_, 8)
        cc = 4 * i + j
        at = xi(cc // 16, (cc // 2) % 8, cc % 2)
        here = (b == r) & (i == b)

        @pl.when(jnp.logical_not(here))
        def _():
            remote(
                xt.at[pl.ds(i * 64, 64)], xb.at[at, :, strip], a_s.at[i], a_r.at[r], (b, cc)
            ).start()

        @pl.when(here)
        def _():
            xb[at, :, strip] = xt[pl.ds(pl.multiple_of(i * 64, 64), 64), :]

    def y_copy(k):
        return remote(yb.at[r], yb.at[r], y_s.at[k], y_r.at[r], (k, c))

    @pl.loop(1, 8)
    def _(i):
        y_copy(lax.rem(r + i, 8)).start()

    @pl.loop(0, 8)
    def _(a):
        @pl.when(jnp.logical_not((a == r) & (r == b)))
        def _():
            remote(
                xt.at[pl.ds(0, 64)], xb.at[own, :, pl.ds(pl.multiple_of(a * 128, 128), 128)],
                a_s.at[0], a_r.at[a], (r, c),
            ).wait_recv()

    def h_copy():
        return remote(xb.at[own], xb.at[own], h_s, h_r, (r, col(1 - y, z, q)))

    def line(sub_):
        return y if sub_ == 0 else 1 - y

    def fwd(at, sems_s, sems_r, n, dev):
        return remote(xb.at[at], xb.at[at], sems_s.at[n], sems_r.at[n], dev)

    up = (r, col(y, lax.rem(z + 1, 8), q))
    down = (r, col(y, lax.rem(z + 7, 8), q))

    def spread(off, sub_, go_up, go_down):
        at = xi(line(sub_), lax.rem(z + off, 8), q)
        if go_up:
            fwd(at, u_s, u_r, ((8 - off) % 8) * 2 + sub_, up).start()
        if go_down:
            fwd(at, v_s, v_r, off * 2 + sub_, down).start()
        fwd(at, s_s, s_r, off * 2 + sub_, sib).start()

    h_copy().start()
    spread(0, 0, True, True)
    remote(xb.at[own], xb.at[xi(1 - y, z, q)], h_s, h_r, (r, c)).wait_recv()
    spread(0, 1, True, True)

    def limits(sub_):
        return 4 - sub_, 3 + sub_

    @pl.loop(1, 8)
    def _(i):
        k = lax.rem(r + 8 - i, 8)
        remote(yb.at[r], yb.at[k], y_s.at[0], y_r.at[k], (r, c)).wait_recv()

    def solve(half):
        cut = pl.ds(half * 256, 256)
        y1 = yb[pl.ds(0, 4), :, cut].reshape(512, 256)
        y2 = yb[pl.ds(4, 4), :, cut].reshape(512, 256)
        z2 = y2.astype(F32) - (dot(fac[0, 0], y1) + dot(fac[0, 1], y1))
        zh, zl = split(z2)
        w1 = dot(fac[2, 0], y1) + dot(fac[2, 1], y1)
        w2 = dot(fac[3, 0], zh) + dot(fac[3, 1], zh) + dot(fac[3, 0], zl)
        wh, wl = split(w2)
        top = w1 - (dot(fac[1, 0], wh) + dot(fac[1, 1], wh) + dot(fac[1, 0], wl))
        wb[pl.ds(0, 512), cut] = top.astype(BF16)
        wb[pl.ds(512, 512), cut] = wh

    solve(0)
    solve(1)

    def finish(off):
        zz = lax.rem(z + off, 8)
        x4 = xb[pl.ds(zz * 4, 4)].reshape(256, 1024)
        delta = dot(x4, wb[...])
        for qq in range(2):
            for yy in range(2):
                row = ((zz % 2) * 2 + qq) * 512 + (yy * 4 + zz // 2) * 64
                rows = pl.ds(pl.multiple_of(row, 64), 64)
                n = (qq * 2 + yy) * 64
                out[rows, :] = (cov[rows, :].astype(F32) - delta[n:n + 64]).astype(BF16)

    def from_sibling(off):
        for sub_ in range(2):
            at = xi(line(sub_), lax.rem(z + off, 8), 1 - q)
            fwd(at, s_s, s_r, off * 2 + sub_, sib).wait_recv()

    from_sibling(0)
    finish(0)
    for d in range(1, 5):
        for sub_ in range(2):
            top_up, top_down = limits(sub_)
            if d <= top_up:
                at = xi(line(sub_), lax.rem(z + 8 - d, 8), q)
                fwd(at, u_s, u_r, (d - 1) * 2 + sub_, up).wait_recv()
                spread(8 - d, sub_, d < top_up, False)
            if d <= top_down:
                at = xi(line(sub_), lax.rem(z + d, 8), q)
                fwd(at, v_s, v_r, (d - 1) * 2 + sub_, down).wait_recv()
                spread(d, sub_, False, d < top_down)
        for off in ((8 - d, d) if d < 4 else (4,)):
            from_sibling(off)
            finish(off)

    @pl.loop(1, 8)
    def _(i):
        k = lax.rem(r + i, 8)
        z_copy(0, i).wait_send()
        zt_copy(0, i).wait_send()
        remote(psend.at[k], rbuf.at[r], r_s.at[k], r_r.at[r], (r, c)).wait_send()
        y_copy(k).wait_send()

    @pl.loop(0, 8)
    def _(i):
        to = 4 * y + lax.rem(z // 2 + i // 2, 4)

        @pl.when(jnp.logical_not((to == r) & (i % 2 == y)))
        def _():
            remote(
                jz.at[pl.ds(0, 2)], jr.at[pl.ds((q * 8 + r) * 2, 2)], p_s.at[i], p_r.at[r], (r, c)
            ).wait_send()

        d_copy(i, q).wait_send()

        @pl.when(jnp.logical_not((b == r) & (i == b)))
        def _():
            remote(xt.at[pl.ds(0, 64)], xb.at[own, :, strip], a_s.at[i], a_r.at[r], (r, c)).wait_send()

    @pl.when(yl == y)
    def _():
        remote(tz.at[pl.ds(0, 2)], tr.at[q], pt_s, pt_r, (r, c)).wait_send()

    dt.wait_send()
    h_copy().wait_send()

    @pl.loop(0, 16)
    def _(n):
        fwd(own, s_s, s_r, n, sib).wait_send()

    @pl.loop(0, 7)
    def _(n):
        fwd(own, u_s, u_r, n, up).wait_send()
        fwd(own, v_s, v_r, jnp.where(n == 6, 7, n), down).wait_send()


def body(cov, jac_blocks, block_positions, block_counts, lower_cross_block, pivot_inverse):
    dma = pltpu.SemaphoreType.DMA
    vmem = pltpu.VMEM
    v_spec = pl.BlockSpec(memory_space=pltpu.VMEM)
    s_spec = pl.BlockSpec(memory_space=pltpu.SMEM)
    return pl.pallas_call(
        kernel,
        out_shape=jax.ShapeDtypeStruct(cov.shape, cov.dtype),
        in_specs=[v_spec, s_spec, s_spec, pl.BlockSpec(memory_space=pl.ANY), v_spec, v_spec],
        out_specs=v_spec,
        scratch_shapes=[
            vmem((2048, 512), BF16),
            vmem((8, 128, 128), BF16),
            vmem((8, 8, 128), jnp.int32),
            vmem((33, 128, 128), BF16),
            vmem((2, 2, 8, 128), jnp.int32),
            pltpu.SMEM((2, 2, 8, 128), jnp.int32),
            vmem((256, 2048), BF16),
            vmem((8, 128, 512), BF16),
            vmem((128, 512), F32),
            vmem((8, 128, 512), BF16),
            vmem((8, 128, 512), BF16),
            vmem((512, 128), BF16),
            vmem((32, 64, 1024), BF16),
            vmem((4, 2, 512, 512), BF16),
            vmem((1024, 512), BF16),
            dma, dma,
            dma((8,)), dma((8,)), dma((8,)), dma((8,)),
            dma((8,)), dma((8,)), dma, dma,
            dma((8,)), dma((8,)), dma, dma,
            dma((8,)), dma((8,)), dma((8,)), dma((8,)),
            dma((8,)), dma((8,)), dma, dma,
            dma((16,)), dma((16,)),
            dma((8,)), dma((8,)), dma((8,)), dma((8,)),
        ],
        compiler_params=pltpu.CompilerParams(
            has_side_effects=True, vmem_limit_bytes=48 * 1024 * 1024
        ),
        cost_estimate=pl.CostEstimate(flops=9 * 2**30, bytes_accessed=8 * 2**20, transcendentals=0),
    )(jac_blocks, block_positions, block_counts, cov, lower_cross_block, pivot_inverse)


def solution(mesh):
    return jax.shard_map(
        body,
        mesh=mesh,
        in_specs=(P("row", "col"), P("col", None, None), P("col", None), P("col"), P(), P()),
        out_specs=P("row", "col"),
        check_vma=False,
    )
```

time: 437 us -> 112 us (0.26)
  the two profiles are of different devices: /device:TPU:8 before, /device:TPU:1 now
where the time goes in v1:
time: 112 us
  Pallas kernels  106 us (95%)
  local copies, waits for them, and re-layouts  5.84 us (5%)
    pallas_call x1, Pallas kernels, body(): pl.pallas_call(kernel, out_shape=jax.ShapeDtypeStruct(cov.shape, cov.dtyp...  106 us
    unnamed x8, local copies, waits for them, and re-layouts  5.84 us

profile of v1, /device:TPU:1, one launch (start us, length us, event | category | flops | bytes accessed | tf_op | source)
XLA Modules:
  0.0 112.0 jit_solution(7151144055933200248)
XLA Ops:
  0.7 0.8 copy.7.pos
  1.4 0.0 copy-start
  1.4 1.6 %copy-done = bf16[2048,512]{1,0:T(8,128)(2,1)S(1)} copy-done((bf16[2048,512]{1,0:T(8,128)(2,1)S(1)}, bf16[2048,512]{1,0:T(8,128)(2,1)}, u32[]{:S(2)}) %copy-start) | copy-done | bytes 2097176
  3.0 0.0 copy-start.1
  3.0 1.2 %copy-done.1 = f32[512,512]{1,0:T(8,128)S(1)} copy-done((f32[512,512]{1,0:T(8,128)S(1)}, f32[512,512]{1,0:T(8,128)}, u32[]{:S(2)}) %copy-start.1) | copy-done | bytes 1048600
  4.2 0.0 copy-start.2
  4.2 0.9 copy-done.2
  5.2 105.5 %shard_map.64 = bf16[2048,512]{1,0:T(8,128)(2,1)S(1)} custom-call(bf16[8,128,128]{2,1,0:T(8,128)(2,1)S(1)} %copy-done.2, s32[8,2]{1,0:T(8,128)S(1)} %copy.7.pos, s32[1]{0:T(128)S(6)} %copy.9.cnt, bf16[2048,512]{1,0:T(8,128)(2,1)S(1)} %copy-done, f32[512,512]{1,0:T(8,128)S(1)} %copy-done.1, f32[2,512,512]{2,1,0:T(8,128)} %pivot.1), custom_call_target="tpu_custom_call" | custom-call | flops 9663676416 | bytes 8388608 | tf_op jit(solution)/shard_map/pallas_call | solution.py:347
  110.7 1.3 %copy.10 = bf16[2048,512]{1,0:T(8,128)(2,1)} copy(bf16[2048,512]{1,0:T(8,128)(2,1)S(1)} %shard_map.64) | data formatting | bytes 4194304
Async XLA Ops:
  1.4 1.6 %copy-start = (bf16[2048,512]{1,0:T(8,128)(2,1)S(1)}, bf16[2048,512]{1,0:T(8,128)(2,1)}, u32[]{:S(2)}) copy-start(bf16[2048,512]{1,0:T(8,128)(2,1)} %cov_hbm.1) | copy-start | bytes 6291460
  3.0 1.2 %copy-start.1 = (f32[512,512]{1,0:T(8,128)S(1)}, f32[512,512]{1,0:T(8,128)}, u32[]{:S(2)}) copy-start(f32[512,512]{1,0:T(8,128)} %lower.1) | copy-start | bytes 3145732
  4.2 0.9 copy-start.2

commit v2 on v0

v2 whole, which is shorter than its diff:
```python
import jax
import jax.numpy as jnp
from jax import lax
from jax.experimental import pallas as pl
from jax.experimental.pallas import tpu as pltpu
from jax.sharding import PartitionSpec as P

MESH = pl.DeviceIdType.MESH
F32 = jnp.float32
BF16 = jnp.bfloat16


def dot(a, b):
    return jnp.dot(a, b, preferred_element_type=F32)


def split(values):
    high = values.astype(BF16)
    return high, (values - high.astype(F32)).astype(BF16)


def kernel(
    jac, pos, cnt, cov_hbm, lower_hbm, pivot_hbm, out,
    cov, ob, lower, pivot, jz, tz, jr, tr, table, lhs, psend, pown, rbuf, yb, xt, xz, xb, fac, wb,
    cov_sem, low_sem, piv_sem, own_sem, tab_sem, out_sem,
    z_s, z_r, zt_s, zt_r, p_s, p_r, pt_s, pt_r, d_s, d_r, dt_s, dt_r,
    r_s, r_r, y_s, y_r, a_s, a_r, b_s, b_r, s_s, s_r, u_s, u_r, v_s, v_r,
):
    r = lax.axis_index("row")
    c = lax.axis_index("col")
    y = c // 16
    z = (c // 2) % 8
    q = c % 2
    yl = r // 4
    x = r % 4
    b = c // 4
    j = c % 4

    def col(y_, z_, q_):
        return (y_ * 8 + z_) * 2 + q_

    def remote(src, dst, ss, rs, dev):
        return pltpu.make_async_remote_copy(
            src_ref=src, dst_ref=dst, send_sem=ss, recv_sem=rs, device_id=dev, device_id_type=MESH
        )

    barrier = pltpu.get_barrier_semaphore()

    def ready(row, col_):
        pl.semaphore_signal(barrier, inc=1, device_id=(row, col_), device_id_type=MESH)

    @pl.loop(1, 8)
    def _(i):
        ready(r, col(y, lax.rem(z + i, 8), q))

    @pl.loop(1, 8)
    def _(i):
        ready(lax.rem(r + i, 8), c)

    @pl.when(yl != y)
    def _():
        @pl.loop(0, 8)
        def _(a):
            ready(a, col(1 - y, z, q))

    ready(r, col(y, z, 1 - q))

    low_copy = pltpu.make_async_copy(lower_hbm, lower, low_sem)
    piv_copy = pltpu.make_async_copy(pivot_hbm, pivot, piv_sem)
    cov_copy = pltpu.make_async_copy(cov_hbm, cov, cov_sem)
    own_copy = pltpu.make_async_copy(jac.at[r], jz.at[z], own_sem)
    own_copy.start()
    low_copy.start()
    piv_copy.start()
    cov_copy.start()

    sub = lax.broadcasted_iota(jnp.int32, (8, 128), 0)
    lane = lax.broadcasted_iota(jnp.int32, (8, 128), 1)
    t = jnp.full((8, 128), 8, jnp.int32)
    for s in range(8):
        hit = (sub == pos[0, s]) & (lane == pos[1, s] - c * 4) & (s < cnt[0])
        t = jnp.where(hit, s, t)
    tz[z] = t
    pl.semaphore_wait(barrier, 19)

    def z_copy(zz, i):
        return remote(jac.at[r], jz.at[z], z_s.at[i], z_r.at[z], (r, col(y, zz, q)))

    def zt_copy(zz, i):
        return remote(tz.at[z], tz.at[z], zt_s.at[i], zt_r.at[z], (r, col(y, zz, q)))

    tables = (yl == y) & (z // 2 == x)

    def near(i):
        return jnp.where(i % 2 == 1, (i + 1) // 2, 8 - i // 2)

    @pl.loop(1, 8)
    def _(i):
        zz = lax.rem(z + near(i), 8)
        z_copy(zz, i).start()

        @pl.when(tables)
        def _():
            zt_copy(zz, i).start()

    jr[32] = jnp.zeros((128, 128), BF16)
    own_copy.wait()

    def p_copy(i, yy, k, zz, dev):
        return remote(
            jz.at[zz], jr.at[(q * 8 + k) * 2 + zz % 2], p_s.at[i, yy], p_r.at[k, zz % 2], dev
        )

    @pl.loop(0, 8)
    def _(i):
        zz = lax.rem(z + jnp.where(i == 0, 0, near(i)), 8)
        to = 4 * y + zz // 2

        @pl.when(i != 0)
        def _():
            remote(jac.at[r], jz.at[zz], z_s.at[0], z_r.at[zz], (r, c)).wait_recv()

            @pl.when(to == r)
            def _():
                remote(tz.at[zz], tz.at[zz], zt_s.at[0], zt_r.at[zz], (r, c)).wait_recv()

        @pl.when(jnp.logical_not((to == r) & (y == 0)))
        def _():
            p_copy(i, 0, r, zz, (to, col(0, z, q))).start()

        @pl.when(jnp.logical_not((to == r) & (y == 1)))
        def _():
            p_copy(i, 1, r, zz, (to, col(1, z, q))).start()

        @pl.when(to == r)
        def _():
            jr[(q * 8 + r) * 2 + zz % 2] = jz[zz]
            tr[q, zz % 2] = tz[zz]

    def pt_copy():
        return remote(
            tr.at[q], tr.at[q], pt_s, pt_r, (r, col(1 - y, z, q))
        )

    @pl.when(yl == y)
    def _():
        pt_copy().start()

    low_copy.wait()
    piv_copy.wait()
    for n, value in enumerate((lower[...], lower[...].T, pivot[0], pivot[1])):
        high, low = split(value)
        fac[n, 0] = high
        fac[n, 1] = low

    sib = (r, col(y, z, 1 - q))

    @pl.when(yl != y)
    def _():
        pt_copy().wait_recv()

    dt = remote(tr.at[q], tr.at[q], dt_s, dt_r, sib)
    dt.start()

    def d_copy(k, side):
        part = jr.at[pl.ds((side * 8 + k) * 2, 2)]
        return remote(part, part, d_s.at[k], d_r.at[k], sib)

    @pl.loop(0, 8)
    def _(i):
        k = lax.rem(r + i, 8)

        @pl.when(jnp.logical_not((k == r) & (yl == y)))
        def _():
            p_copy(0, 0, k, 0, (r, c)).wait_recv()
            p_copy(0, 0, k, 1, (r, c)).wait_recv()

        d_copy(k, q).start()

    remote(tr.at[q], tr.at[1 - q], dt_s, dt_r, sib).wait_recv()
    tab_copy = pltpu.make_async_copy(tr, table, tab_sem)
    tab_copy.start()
    tab_copy.wait()

    @pl.loop(0, 8)
    def _(k):
        d_copy(k, 1 - q).wait_recv()


    @pl.loop(0, 8)
    def _(k):
        for bb in range(2):
            for qq in range(2):
                for l in range(4):
                    at = table[qq, bb, k, l]
                    at = jnp.where(at < 8, (qq * 8 + at) * 2 + bb, 32)
                    place = ((2 * bb + qq) * 4 + l) * 128
                    lhs[k, :, place:place + 128] = jr[at]

    cov_copy.wait()

    for g in range(2):

        @pl.loop(0, 4)
        def _(i):
            pair = lax.rem(r // 2 + 1 + i, 4)
            part = dot(
                lhs[pl.ds(2 * pair, 2)].reshape(256, 2048), cov[:, g * 256:(g + 1) * 256]
            )
            for h in range(2):
                k = 2 * pair + h

                @pl.when(k == r)
                def _():
                    pown[g] = part[h * 128:(h + 1) * 128]

                @pl.when(k != r)
                def _():
                    psend[g, k] = part[h * 128:(h + 1) * 128].astype(BF16)
                    remote(
                        psend.at[g, k], rbuf.at[g, r], r_s.at[g, k], r_r.at[g, r], (k, c)
                    ).start()


    def block(zz, qq):
        return pl.ds((lax.rem(zz, 4) * 2 + qq) * 4, 4)

    def half(zz, qq, yy):
        return pl.ds(((lax.rem(zz, 4) * 2 + qq) * 2 + yy) * 2, 2)

    def strip(a):
        return pl.ds(pl.multiple_of(a * 128, 128), 128)

    def a_copy(g, i, dev):
        return remote(
            xt.at[g, lax.rem(i, 2)], xz.at[g, z // 2], a_s.at[g, i], a_r.at[g, z // 2], dev
        )

    def b_copy(g, n, yy, dev):
        return remote(
            xz.at[g, n], xb.at[g, block(z, q), :, strip(r)],
            b_s.at[g, n, yy], b_r.at[g, r], dev,
        )

    def y_copy(g, k):
        return remote(yb.at[g, r], yb.at[g, r], y_s.at[g, k], y_r.at[g, r], (k, c))

    def total(g):
        @pl.loop(1, 8)
        def _(i):
            k = lax.rem(r + 8 - i, 8)
            remote(psend.at[g, 0], rbuf.at[g, k], r_s.at[g, 0], r_r.at[g, k], (r, c)).wait_recv()
            pown[g] += rbuf[g, k].astype(F32)

        mine = pown[g]
        yb[g, r] = mine.astype(BF16)
        turned = mine.T.astype(BF16).reshape(2, 4, 32, 128)
        for i in range(4):
            for yy in range(2):
                xt[g, i % 2, yy * 2 + i // 2] = turned[yy, i]
        xz[g, z // 2] = xt[g, (z // 2) % 2]

        for n in range(1, 4):
            i = lax.rem(z // 2 + n, 4)
            a_copy(g, i, (r, col(y, i * 2 + z % 2, q))).start()

    def turn(g):
        for n_ in range(4):
            n = lax.rem(z // 2 + (0, 1, 3, 2)[n_], 4)
            if n_ > 0:
                remote(xt.at[g, 0], xz.at[g, n], a_s.at[g, 0], a_r.at[g, n], (r, c)).wait_recv()
            to = 4 * y + n
            for yy in range(2):
                here = (to == r) & (yy == y)

                @pl.when(jnp.logical_not(here))
                def _():
                    b_copy(g, n, yy, (to, col(yy, z, q))).start()

                @pl.when(here)
                def _():
                    xb[g, block(z, q), :, strip(r)] = xz[g, n]

    def to_rows(g):
        @pl.loop(1, 8)
        def _(i):
            y_copy(g, lax.rem(r + i, 8)).start()

    def fwd(g, zz, qq, yy, sems_s, sems_r, n, dev):
        part = xb.at[g, half(zz, qq, yy)]
        return remote(part, part, sems_s.at[g, n], sems_r.at[g, n], dev)

    up = (r, col(y, lax.rem(z + 1, 8), q))
    down = (r, col(y, lax.rem(z + 7, 8), q))

    def go_up(g, d, yy):
        return fwd(g, z + 4 - d, q, yy, u_s, u_r, d * 2 + yy, up)

    def go_down(g, d, yy):
        return fwd(g, z + d, q, yy, v_s, v_r, d * 2 + yy, down)

    def over(g, d, yy, qq):
        return fwd(g, z + d, qq, yy, s_s, s_r, d * 2 + yy, sib)

    def held(g):
        @pl.loop(0, 8)
        def _(a):
            @pl.when(jnp.logical_not((a == r) & (yl == y)))
            def _():
                remote(
                    xz.at[g, 0], xb.at[g, block(z, q), :, strip(a)],
                    b_s.at[g, 0, 0], b_r.at[g, a], (r, c),
                ).wait_recv()

        go_up(g, 0, 0).start()
        go_down(g, 0, 1).start()
        go_up(g, 0, 1).start()
        go_down(g, 0, 0).start()
        over(g, 0, 0, q).start()
        over(g, 0, 1, q).start()

    def came_up(g, d, yy):
        fwd(g, z + 4 - d, q, yy, u_s, u_r, (d - 1) * 2 + yy, up).wait_recv()

    def came_down(g, d, yy):
        fwd(g, z + d, q, yy, v_s, v_r, (d - 1) * 2 + yy, down).wait_recv()

    def ring1(g):
        came_up(g, 1, 0)
        go_up(g, 1, 0).start()
        over(g, 3, 0, q).start()
        came_down(g, 1, 1)
        go_down(g, 1, 1).start()
        over(g, 1, 1, q).start()

    def ring2(g):
        came_up(g, 1, 1)
        over(g, 3, 1, q).start()
        came_down(g, 1, 0)
        over(g, 1, 0, q).start()

    def ring3(g):
        came_up(g, 2, 0)
        over(g, 2, 0, q).start()
        came_down(g, 2, 1)
        over(g, 2, 1, q).start()

    def solve(g):
        @pl.loop(1, 8)
        def _(i):
            k = lax.rem(r + 8 - i, 8)
            remote(yb.at[g, r], yb.at[g, k], y_s.at[g, 0], y_r.at[g, k], (r, c)).wait_recv()

        cut = pl.ds(g * 256, 256)
        y1 = yb[g, 0:4].reshape(512, 256)
        y2 = yb[g, 4:8].reshape(512, 256)
        z2 = y2.astype(F32) - (dot(fac[0, 0], y1) + dot(fac[0, 1], y1))
        zh, zl = split(z2)
        w1 = dot(fac[2, 0], y1) + dot(fac[2, 1], y1)
        w2 = dot(fac[3, 0], zh) + dot(fac[3, 1], zh) + dot(fac[3, 0], zl)
        wh, wl = split(w2)
        top = w1 - (dot(fac[1, 0], wh) + dot(fac[1, 1], wh) + dot(fac[1, 0], wl))
        wb[pl.ds(0, 512), cut] = top.astype(BF16)
        wb[pl.ds(512, 512), cut] = wh

    def finish(g, off):
        for yy in range(2):
            over(g, off, yy, 1 - q).wait_recv()

        zz = lax.rem(z + off, 4)
        x8 = xb[g, pl.ds(zz * 8, 8)].reshape(256, 1024)
        delta = dot(x8, wb[...])
        for qq in range(2):
            for yy in range(2):
                for m in range(2):
                    row = ((zz % 2) * 2 + qq) * 512 + g * 256 + (yy * 4 + m * 2 + zz // 2) * 32
                    rows = pl.ds(pl.multiple_of(row, 32), 32)
                    n = ((qq * 2 + yy) * 2 + m) * 32
                    ob[rows, :] = (cov[rows, :].astype(F32) - delta[n:n + 32]).astype(BF16)

    def out_copy(g, n):
        rows = pl.ds(n * 512 + g * 256, 256)
        return pltpu.make_async_copy(ob.at[rows], out.at[rows], out_sem.at[g, n])

    def store(g):
        for n in range(4):
            out_copy(g, n).start()

    total(0)
    turn(0)
    total(1)
    held(0)
    turn(1)
    to_rows(0)
    to_rows(1)
    ring1(0)
    held(1)
    ring2(0)
    ring3(0)
    ring1(1)
    solve(0)
    ring2(1)
    solve(1)
    for off in range(4):
        finish(0, off)
    store(0)
    finish(1, 0)
    ring3(1)
    for off in (1, 3, 2):
        finish(1, off)
    store(1)

    @pl.loop(1, 8)
    def _(i):
        z_copy(0, i).wait_send()

        @pl.when(tables)
        def _():
            zt_copy(0, i).wait_send()

    for g in range(2):

        @pl.loop(1, 8)
        def _(i):
            k = lax.rem(r + i, 8)
            remote(psend.at[g, k], rbuf.at[g, r], r_s.at[g, k], r_r.at[g, r], (r, c)).wait_send()
            y_copy(g, k).wait_send()

        for n in range(1, 4):
            a_copy(g, lax.rem(z // 2 + n, 4), (r, c)).wait_send()

        @pl.loop(0, 4)
        def _(n):
            for yy in range(2):

                @pl.when(jnp.logical_not((4 * y + n == r) & (yy == y)))
                def _():
                    b_copy(g, n, yy, (r, c)).wait_send()

        for d in range(4):
            for yy in range(2):
                over(g, d, yy, q).wait_send()
        for d, yy in ((0, 0), (0, 1), (1, 0)):
            go_up(g, d, yy).wait_send()
            go_down(g, d, yy if d == 0 else 1).wait_send()

        for n in range(4):
            out_copy(g, n).wait()

    @pl.loop(0, 8)
    def _(i):
        zz = lax.rem(z + jnp.where(i == 0, 0, near(i)), 8)
        for yy in range(2):

            @pl.when(jnp.logical_not((4 * y + zz // 2 == r) & (y == yy)))
            def _():
                p_copy(i, yy, r, zz, (r, c)).wait_send()

        d_copy(i, q).wait_send()

    @pl.when(yl == y)
    def _():
        pt_copy().wait_send()

    dt.wait_send()


def body(cov, jac_blocks, block_positions, block_counts, lower_cross_block, pivot_inverse):
    dma = pltpu.SemaphoreType.DMA
    vmem = pltpu.VMEM
    h_spec = pl.BlockSpec(memory_space=pltpu.HBM)
    a_spec = pl.BlockSpec(memory_space=pl.ANY)
    s_spec = pl.BlockSpec(memory_space=pltpu.SMEM)
    return pl.pallas_call(
        kernel,
        out_shape=jax.ShapeDtypeStruct(cov.shape, cov.dtype),
        in_specs=[h_spec, s_spec, s_spec, h_spec, h_spec, h_spec],
        out_specs=a_spec,
        scratch_shapes=[
            vmem((2048, 512), BF16),
            vmem((2048, 512), BF16),
            vmem((512, 512), F32),
            vmem((2, 512, 512), F32),
            vmem((8, 128, 128), BF16),
            vmem((8, 8, 128), jnp.int32),
            vmem((33, 128, 128), BF16),
            vmem((2, 2, 8, 128), jnp.int32),
            pltpu.SMEM((2, 2, 8, 128), jnp.int32),
            vmem((8, 128, 2048), BF16),
            vmem((2, 8, 128, 256), BF16),
            vmem((2, 128, 256), F32),
            vmem((2, 8, 128, 256), BF16),
            vmem((2, 8, 128, 256), BF16),
            vmem((2, 2, 4, 32, 128), BF16),
            vmem((2, 4, 4, 32, 128), BF16),
            vmem((2, 32, 32, 1024), BF16),
            vmem((4, 2, 512, 512), BF16),
            vmem((1024, 512), BF16),
            dma, dma, dma, dma, dma, dma((2, 4)),
            dma((8,)), dma((8,)), dma((8,)), dma((8,)),
            dma((8, 2)), dma((8, 2)), dma, dma,
            dma((8,)), dma((8,)), dma, dma,
            dma((2, 8)), dma((2, 8)), dma((2, 8)), dma((2, 8)),
            dma((2, 4)), dma((2, 4)), dma((2, 4, 2)), dma((2, 8)),
            dma((2, 8)), dma((2, 8)),
            dma((2, 4)), dma((2, 4)), dma((2, 4)), dma((2, 4)),
        ],
        compiler_params=pltpu.CompilerParams(
            collective_id=0, has_side_effects=True, vmem_limit_bytes=62 * 1024 * 1024
        ),
        cost_estimate=pl.CostEstimate(flops=9 * 2**30, bytes_accessed=8 * 2**20, transcendentals=0),
    )(jac_blocks, block_positions.T, block_counts, cov, lower_cross_block, pivot_inverse)


def solution(mesh):
    return jax.shard_map(
        body,
        mesh=mesh,
        in_specs=(P("row", "col"), P("col", None, None), P("col", None), P("col"), P(), P()),
        out_specs=P("row", "col"),
        check_vma=False,
    )
```

time: 437 us -> 85.2 us (0.19)
  the two profiles are of different devices: /device:TPU:8 before, /device:TPU:1 now
where the time goes in v2:
time: 85.2 us; the launch traced here: 84.7 us
  Pallas kernels  81 us (95%)
  local copies, waits for them, and re-layouts  3.05 us (4%)
    pallas_call x1, Pallas kernels, body(): pl.pallas_call(kernel, out_shape=jax.ShapeDtypeStruct(cov.shape, cov.dtyp...  81 us
    unnamed x1, local copies, waits for them, and re-layouts  3.05 us

profile of v2, /device:TPU:1, one launch (start us, length us, event | category | flops | bytes accessed | tf_op | source)
XLA Modules:
  0.0 84.7 jit_solution(523238247466728094)
XLA Ops:
  0.7 81.0 %shard_map.64 = bf16[2048,512]{1,0:T(8,128)(2,1)} custom-call(bf16[8,128,128]{2,1,0:T(8,128)(2,1)} %jac.1, s32[2,8]{1,0:T(2,128)} %bitcast.1, s32[1]{0:T(128)S(6)} %copy.8.cnt, bf16[2048,512]{1,0:T(8,128)(2,1)} %cov_hbm.1, f32[512,512]{1,0:T(8,128)} %lower_hbm.1, f32[2,512,512]{2,1,0:T(8,128)} %pivot_hbm.1), custom_call_target="tpu_custom_call" | custom-call | flops 9663676416 | bytes 8388608 | tf_op jit(solution)/shard_map/pallas_call | solution.py:474
  81.6 3.0 %copy.9 = bf16[2048,512]{1,0:T(8,128)(2,1)} copy(bf16[2048,512]{1,0:T(8,128)(2,1)} %shard_map.64) | data formatting | bytes 4194304

commit v3 on v2

--- a/solution.py
+++ b/solution.py
@@ -44,27 +44,6 @@
             src_ref=src, dst_ref=dst, send_sem=ss, recv_sem=rs, device_id=dev, device_id_type=MESH
         )
 
-    barrier = pltpu.get_barrier_semaphore()
-
-    def ready(row, col_):
-        pl.semaphore_signal(barrier, inc=1, device_id=(row, col_), device_id_type=MESH)
-
-    @pl.loop(1, 8)
-    def _(i):
-        ready(r, col(y, lax.rem(z + i, 8), q))
-
-    @pl.loop(1, 8)
-    def _(i):
-        ready(lax.rem(r + i, 8), c)
-
-    @pl.when(yl != y)
-    def _():
-        @pl.loop(0, 8)
-        def _(a):
-            ready(a, col(1 - y, z, q))
-
-    ready(r, col(y, z, 1 - q))
-
     low_copy = pltpu.make_async_copy(lower_hbm, lower, low_sem)
     piv_copy = pltpu.make_async_copy(pivot_hbm, pivot, piv_sem)
     cov_copy = pltpu.make_async_copy(cov_hbm, cov, cov_sem)
@@ -74,6 +53,23 @@
     piv_copy.start()
     cov_copy.start()
 
+    barrier = pltpu.get_barrier_semaphore()
+
+    def ready(row, col_):
+        pl.semaphore_signal(barrier, inc=1, device_id=(row, col_), device_id_type=MESH)
+
+    @pl.loop(1, 8)
+    def _(i):
+        ready(r, col(y, lax.rem(z + i, 8), q))
+
+    @pl.loop(0, 8)
+    def _(a):
+        @pl.when(jnp.logical_not((a == r) & (yl == y)))
+        def _():
+            ready(a, col(yl, z, q))
+
+    ready(r, col(y, z, 1 - q))
+
     sub = lax.broadcasted_iota(jnp.int32, (8, 128), 0)
     lane = lax.broadcasted_iota(jnp.int32, (8, 128), 1)
     t = jnp.full((8, 128), 8, jnp.int32)
@@ -81,7 +77,7 @@
         hit = (sub == pos[0, s]) & (lane == pos[1, s] - c * 4) & (s < cnt[0])
         t = jnp.where(hit, s, t)
     tz[z] = t
-    pl.semaphore_wait(barrier, 19)
+    pl.semaphore_wait(barrier, jnp.where(yl == y, 15, 16))
 
     def z_copy(zz, i):
         return remote(jac.at[r], jz.at[z], z_s.at[i], z_r.at[z], (r, col(y, zz, q)))
@@ -187,8 +183,7 @@
         d_copy(k, 1 - q).wait_recv()
 
 
-    @pl.loop(0, 8)
-    def _(k):
+    def dense(k):
         for bb in range(2):
             for qq in range(2):
                 for l in range(4):
@@ -199,11 +194,17 @@
 
     cov_copy.wait()
 
+    def r_copy(g, k):
+        return remote(psend.at[g, k], rbuf.at[g, r], r_s.at[g, k], r_r.at[g, r], (k, c))
+
     for g in range(2):
 
         @pl.loop(0, 4)
         def _(i):
             pair = lax.rem(r // 2 + 1 + i, 4)
+            if g == 0:
+                dense(2 * pair)
+                dense(2 * pair + 1)
             part = dot(
                 lhs[pl.ds(2 * pair, 2)].reshape(256, 2048), cov[:, g * 256:(g + 1) * 256]
             )
@@ -217,9 +218,16 @@
                 @pl.when(k != r)
                 def _():
                     psend[g, k] = part[h * 128:(h + 1) * 128].astype(BF16)
-                    remote(
-                        psend.at[g, k], rbuf.at[g, r], r_s.at[g, k], r_r.at[g, r], (k, c)
-                    ).start()
+                    if g == 0:
+                        r_copy(g, k).start()
+
+    @pl.loop(1, 8)
+    def _(i):
+        r_copy(0, lax.rem(r + i, 8)).wait_send()
+
+    @pl.loop(1, 8)
+    def _(i):
+        r_copy(1, lax.rem(r + i, 8)).start()
 
 
     def block(zz, qq):
@@ -389,18 +397,18 @@
     total(0)
     turn(0)
     total(1)
+    to_rows(0)
     held(0)
     turn(1)
-    to_rows(0)
-    to_rows(1)
     ring1(0)
     held(1)
+    to_rows(1)
     ring2(0)
     ring3(0)
+    solve(0)
     ring1(1)
-    solve(0)
+    solve(1)
     ring2(1)
-    solve(1)
     for off in range(4):
         finish(0, off)
     store(0)
@@ -423,7 +431,8 @@
         @pl.loop(1, 8)
         def _(i):
             k = lax.rem(r + i, 8)
-            remote(psend.at[g, k], rbuf.at[g, r], r_s.at[g, k], r_r.at[g, r], (r, c)).wait_send()
+            if g == 1:
+                r_copy(g, k).wait_send()
             y_copy(g, k).wait_send()
 
         for n in range(1, 4):

time: 85.2 us -> 83.6 us (0.981)
  Pallas kernels: 81 us -> 79.8 us
    pallas_call x1, Pallas kernels: 81 us -> 79.8 us  [body(): pl.pallas_call(kernel, out_shape=jax.ShapeDtypeStruct(cov.shape, cov.dtyp...]
where the time goes in v3:
time: 83.6 us; the launch traced here: 83.5 us
  Pallas kernels  79.8 us (95%)
  local copies, waits for them, and re-layouts  3.05 us (4%)
    pallas_call x1, Pallas kernels, body(): pl.pallas_call(kernel, out_shape=jax.ShapeDtypeStruct(cov.shape, cov.dtyp...  79.8 us
    unnamed x1, local copies, waits for them, and re-layouts  3.05 us

profile of v3, /device:TPU:1, one launch (start us, length us, event | category | flops | bytes accessed | tf_op | source)
XLA Modules:
  0.0 83.5 jit_solution(12417887755543486440)
XLA Ops:
  0.7 79.8 %shard_map.64 = bf16[2048,512]{1,0:T(8,128)(2,1)} custom-call(bf16[8,128,128]{2,1,0:T(8,128)(2,1)} %jac.1, s32[2,8]{1,0:T(2,128)} %bitcast.1, s32[1]{0:T(128)S(6)} %copy.8.cnt, bf16[2048,512]{1,0:T(8,128)(2,1)} %cov_hbm.1, f32[512,512]{1,0:T(8,128)} %lower_hbm.1, f32[2,512,512]{2,1,0:T(8,128)} %pivot_hbm.1), custom_call_target="tpu_custom_call" | custom-call | flops 9663676416 | bytes 8388608 | tf_op jit(solution)/shard_map/pallas_call | solution.py:483
  80.4 3.0 %copy.9 = bf16[2048,512]{1,0:T(8,128)(2,1)} copy(bf16[2048,512]{1,0:T(8,128)(2,1)} %shard_map.64) | data formatting | bytes 4194304

commit v4 on v3

--- a/solution.py
+++ b/solution.py
@@ -387,7 +387,7 @@
                     ob[rows, :] = (cov[rows, :].astype(F32) - delta[n:n + 32]).astype(BF16)
 
     def out_copy(g, n):
-        rows = pl.ds(n * 512 + g * 256, 256)
+        rows = pl.ds(pl.multiple_of(n * 512 + g * 256, 256), 256)
         return pltpu.make_async_copy(ob.at[rows], out.at[rows], out_sem.at[g, n])
 
     def store(g):
@@ -414,9 +414,13 @@
     store(0)
     finish(1, 0)
     ring3(1)
-    for off in (1, 3, 2):
+    for off in (1, 3):
         finish(1, off)
-    store(1)
+    for qq in range(2):
+        out_copy(1, lax.rem(z + 1, 2) * 2 + qq).start()
+    finish(1, 2)
+    for qq in range(2):
+        out_copy(1, lax.rem(z, 2) * 2 + qq).start()
 
     @pl.loop(1, 8)
     def _(i):

time: 83.6 us -> 83.4 us (level)
  no operation moved by 1% of the time
where the time goes in v4:
time: 83.4 us; the launch traced here: 83.3 us
  Pallas kernels  79.6 us (95%)
  local copies, waits for them, and re-layouts  3.05 us (4%)
    pallas_call x1, Pallas kernels, body(): pl.pallas_call(kernel, out_shape=jax.ShapeDtypeStruct(cov.shape, cov.dtyp...  79.6 us
    unnamed x1, local copies, waits for them, and re-layouts  3.05 us

profile of v4, /device:TPU:1, one launch (start us, length us, event | category | flops | bytes accessed | tf_op | source)
XLA Modules:
  0.0 83.3 jit_solution(534465087214550265)
XLA Ops:
  0.7 79.6 %shard_map.64 = bf16[2048,512]{1,0:T(8,128)(2,1)} custom-call(bf16[8,128,128]{2,1,0:T(8,128)(2,1)} %jac.1, s32[2,8]{1,0:T(2,128)} %bitcast.1, s32[1]{0:T(128)S(6)} %copy.8.cnt, bf16[2048,512]{1,0:T(8,128)(2,1)} %cov_hbm.1, f32[512,512]{1,0:T(8,128)} %lower_hbm.1, f32[2,512,512]{2,1,0:T(8,128)} %pivot_hbm.1), custom_call_target="tpu_custom_call" | custom-call | flops 9663676416 | bytes 8388608 | tf_op jit(solution)/shard_map/pallas_call | solution.py:487
  80.3 3.0 %copy.9 = bf16[2048,512]{1,0:T(8,128)(2,1)} copy(bf16[2048,512]{1,0:T(8,128)(2,1)} %shard_map.64) | data formatting | bytes 4194304
